TPU v7x, 32 devices: a whole 2x2x4 slice. The times are simulated.
32 devices in a mesh: feat: 4 (over x, core), work: 8 (over z, y).
Axes of the slice: x: 2, y: 2, z: 4, core: 2. Of those that a mesh axis runs over, the one named last changes fastest.
Arguments:
- momentum: bfloat16 [8, 8192, 1024], P('work', 'feat'), may hold values from -6 to 6
- gradient: bfloat16 [8, 8192, 1024], P('work', 'feat'), may hold values from -6 to 6
- weight: bfloat16 [8192, 1024], P('feat'), may hold values from -3 to 3
- tokens: bfloat16 [8192, 8192], P('work', 'feat'), may hold values from -6 to 6
- select: int32 [8, 64, 8, 4], P('work', 'feat'), may hold values from 0 to 127, as said below
Outputs:
- moment_out: bfloat16 [8, 8192, 1024], P('work', 'feat')
- weight_out: bfloat16 [8192, 1024], P('feat')
- projected: bfloat16 [8192, 1024], P('work', 'feat')
Inputs may be any that keep to these rules, and one draw needn't show every extreme that they name: `select`: for each worker and tile the 4 indices are distinct.
All inputs are finite; a program needn't handle non-finite values.
Results may differ from a plain program's by a relative error of at most 0.015.
Values may be sent and summed in bfloat16 or wider, within the bound.
A program may use at most 128 MiB of HBM per device.

v0:
```python
import math

import jax
import jax.numpy as jnp
from jax import lax
from jax.sharding import PartitionSpec as P

D = 8192
TILE = 128


HIGHEST_PRECISION = lax.Precision.HIGHEST
DECAY = 0.9
RATE = 8.0


def cosine_basis(order):
    freq = jnp.arange(order, dtype=jnp.int32).astype(jnp.float32)[:, None]
    place = jnp.arange(order, dtype=jnp.int32).astype(jnp.float32)[None, :]
    scale = jnp.where(freq == 0.0, math.sqrt(1.0 / order), math.sqrt(2.0 / order))
    return scale * jnp.cos(math.pi * (2.0 * place + 1.0) * freq / (2.0 * order))


def local(momentum, gradient, weight, tokens, select):
    transform = cosine_basis(TILE)
    local_rows, out_width = weight.shape
    row_tiles = local_rows // TILE
    col_tiles = out_width // TILE
    workers = lax.axis_size("work")
    positions = jnp.arange(TILE, dtype=jnp.int32)
    chosen = select[0]
    blended = (DECAY * momentum[0].astype(jnp.float32) + gradient[0].astype(jnp.float32)).reshape(
        row_tiles, TILE, col_tiles, TILE
    )
    onehot = (chosen[..., None] == positions).astype(jnp.float32)
    rows_basis = jnp.einsum("abkr,rj->abkj", onehot, transform, precision=HIGHEST_PRECISION)
    partial_value = jnp.einsum("abkr,arbc->akbc", rows_basis, blended, precision=HIGHEST_PRECISION)
    decoded = jnp.einsum("abkr,akbc->arbc", rows_basis, partial_value, precision=HIGHEST_PRECISION)
    moment_out = (blended - decoded).reshape(local_rows, out_width).astype(jnp.bfloat16)[None]
    row_marks = jnp.arange(TILE, dtype=jnp.int32).astype(jnp.float32)
    initial = jnp.zeros((row_tiles, TILE, col_tiles, TILE), jnp.float32)
    values = lax.all_gather(
        partial_value[None].astype(jnp.bfloat16), "work", axis=0, tiled=True
    ).astype(jnp.float32)
    locations = lax.all_gather(
        chosen.astype(jnp.float32)[None].astype(jnp.bfloat16), "work", axis=0, tiled=True
    ).astype(jnp.float32)
    indicator = (locations[..., None] == row_marks).astype(jnp.float32)
    summed = initial + jnp.einsum(
        "nabkr,nakbc->arbc", indicator, values, precision=HIGHEST_PRECISION
    )
    weight_out = (
        weight.astype(jnp.float32)
        - RATE
        * jnp.einsum(
            "rj,arbc->ajbc", transform, summed / workers, precision=HIGHEST_PRECISION
        ).reshape(local_rows, out_width)
    ).astype(jnp.bfloat16)
    summed_out = lax.psum_scatter(
        lax.dot_general(
            weight_out, tokens, (((0,), (1,)), ((), ())), preferred_element_type=jnp.float32
        ).astype(jnp.bfloat16),
        "feat",
        scatter_dimension=0,
        tiled=True,
    ).astype(jnp.float32)
    projected = (summed_out.T * (1.0 / math.sqrt(D))).astype(jnp.bfloat16)
    return (moment_out, weight_out, projected)


def solution(mesh):
    in_specs = (
        P("work", "feat", None),
        P("work", "feat", None),
        P("feat", None),
        P("work", "feat"),
        P("work", "feat", None, None),
    )
    out_specs = (P("work", "feat", None), P("feat", None), P("work", "feat"))
    return jax.shard_map(local, mesh=mesh, in_specs=in_specs, out_specs=out_specs, check_vma=False)
```

profile of v0, /device:TPU:0, one launch (start us, length us, event | category | flops | bytes accessed | tf_op | source)
XLA Modules:
  0.0 166.0 jit_solution(15831966459224031147)
XLA Ops:
  7.2 0.0 all-gather.3.cloned.1.call-start
  7.2 0.8 copy.35
  8.0 0.1 iota_compare_fusion
  8.2 5.5 %add_bitcast_fusion = f32[256,8,8,128]{3,1,2,0:T(8,128)S(1)} fusion(bf16[1,2048,1024]{2,1,0:T(8,128)(2,1)} %param.6, bf16[1,2048,1024]{2,1,0:T(8,128)(2,1)} %param.5), kind=kLoop, calls=%fused_computation.8 | loop fusion | flops 8388608 | bytes 16777216
  13.7 5.3 %copy.54 = f32[256,8,8,128]{3,2,1,0:T(8,128)} copy(f32[256,8,8,128]{3,1,2,0:T(8,128)S(1)} %add_bitcast_fusion) | data formatting | bytes 16777216
  19.0 9.3 %copy.39 = f32[16,128,8,128]{1,3,2,0:T(8,128)} copy(f32[16,128,8,128]{3,2,1,0:T(8,128)} %bitcast.51) | data formatting | bytes 16777216 | tf_op jit(solution)/shard_map/add | solution.py:32
  28.3 0.6 fusion.11
  28.9 15.4 %fusion.27 = (bf16[16,4,8,128]{3,1,2,0:T(4,128)(2,1)S(1)}, f32[16,4,8,128]{3,1,2,0:T(4,128)S(1)}) fusion(f32[16,128,8,128]{1,3,2,0:T(8,128)} %copy.39, f32[16,8,4,128]{3,2,1,0:T(4,128)S(1)} %fusion.11), kind=kOutput, calls=%fused_computation.40 | convolution fusion | flops 100728832 | bytes 9043968 | tf_op jit(solution)/shard_map/abkr,arbc->akbc/dot_general | solution.py:37
  44.2 0.7 copy.41
  45.0 0.0 reduce-scatter.2.cloned.1.call-start
  45.0 32.6 %all_gather.7 = bf16[8,16,8,4]{1,2,3,0:T(8,128)(2,1)S(1)} all-gather(bf16[1,16,8,4]{1,2,3,0:T(8,128)(2,1)S(1)} %fusion.23), channel_id=1, replica_groups=mesh['feat'=4,'work'=8] {'work'}, dimensions={0}, use_global_device_ids=true | all-gather | bytes 9216 | tf_op jit(solution)/shard_map/all_gather | solution.py:45
  77.7 0.5 copy.43
  78.2 9.9 %all-gather.3.cloned.1.call-done = bf16[128,4,8,128]{3,2,1,0:T(8,128)(2,1)} async-done(((bf16[16,4,8,128]{3,2,1,0:T(8,128)(2,1)}), bf16[128,4,8,128]{3,2,1,0:T(8,128)(2,1)}) %all-gather.3.cloned.1.call-update) | async-done | bytes 1048592 | tf_op jit(solution)/shard_map/all_gather | solution.py:42
  88.1 4.8 %fusion.7 = f32[16,8,128,128,1]{3,2,4,1,0:T(8,128)S(1)} fusion(bf16[8,16,4,8,128]{4,3,2,1,0:T(8,128)(2,1)} %bitcast.54, f32[128]{0:T(128)S(1)} %iota_convert_fusion, f32[8,16,8,4]{3,2,1,0:T(8,128)S(1)} %copy.43), kind=kOutput, calls=%fused_computation.10 | convolution fusion | flops 134742016 | bytes 9454080 | tf_op jit(solution)/shard_map/nabkr,nakbc->arbc/dot_general | solution.py:49
  92.9 9.5 %multiply_bitcast_fusion = f32[16,128,8,128]{1,3,2,0:T(8,128)} fusion(f32[16,8,128,128,1]{3,2,4,1,0:T(8,128)S(1)} %fusion.7, f32[128]{0:T(128)S(1)} %iota_convert_fusion, f32[128]{0:T(128)S(1)} %get-tuple-element.18, f32[128]{0:T(128)S(1)} %get-tuple-element.17), kind=kOutput, calls=%fused_computation.7 | convolution fusion | flops 3225468928 | bytes 16778752 | tf_op jit(solution)/shard_map/rj,arbc->ajbc/dot_general | solution.py:55
  102.4 9.3 %copy.45 = f32[16,128,8,128]{3,2,1,0:T(8,128)} copy(f32[16,128,8,128]{1,3,2,0:T(8,128)} %multiply_bitcast_fusion) | data formatting | bytes 16777216 | tf_op jit(solution)/shard_map/mul | solution.py:54
  111.6 6.9 %fusion = bf16[2048,1024]{1,0:T(8,128)(2,1)S(1)} fusion(f32[256,8,8,128]{3,2,1,0:T(8,128)} %bitcast.52, bf16[2048,1024]{1,0:T(8,128)(2,1)} %param.7), kind=kLoop, calls=%fused_computation.1 | loop fusion | flops 6291456 | bytes 16777216 | tf_op jit(solution)/shard_map/convert_element_type | solution.py:58
  118.6 2.0 %copy-done = bf16[2048,1024]{1,0:T(8,128)(2,1)} copy-done((bf16[2048,1024]{1,0:T(8,128)(2,1)}, bf16[2048,1024]{1,0:T(8,128)(2,1)S(1)}, u32[]{:S(2)}) %copy-start) | copy-done | bytes 4194328
  120.6 5.8 %convolution_convert_fusion = bf16[1024,1024]{1,0:T(8,128)(2,1)} fusion(bf16[2048,1024]{1,0:T(8,128)(2,1)S(1)} %fusion, bf16[1024,2048]{1,0:T(8,128)(2,1)S(1)} %copy-done.2), kind=kOutput, calls=%fused_computation.12 | convolution fusion | flops 4296015872 | bytes 10485760 | tf_op jit(solution)/shard_map/dot_general | solution.py:60
  126.4 16.6 %fusion.3 = bf16[16,128,8,128]{1,3,2,0:T(8,128)(2,1)} fusion(f32[16,128,8,128]{1,3,2,0:T(8,128)} %copy.39, f32[16,4,8,128]{3,1,2,0:T(4,128)S(1)} %get-tuple-element.16, f32[16,8,4,128]{3,2,1,0:T(4,128)S(1)} %fusion.11), kind=kOutput, calls=%fused_computation.6 | convolution fusion | flops 104857600 | bytes 13107200 | tf_op jit(solution)/shard_map/abkr,akbc->arbc/dot_general | solution.py:38
  143.0 6.7 %copy.40 = bf16[16,128,8,128]{3,2,1,0:T(8,128)(2,1)} copy(bf16[16,128,8,128]{1,3,2,0:T(8,128)(2,1)} %fusion.3) | data formatting | bytes 8388608 | tf_op jit(solution)/shard_map/convert_element_type | solution.py:39
  149.7 7.3 %convert_element_type.90 = bf16[1,2048,1024]{2,1,0:T(8,128)(2,1)} reshape(bf16[16,128,8,128]{3,2,1,0:T(8,128)(2,1)} %copy.40) | data formatting | bytes 8388608 | tf_op jit(solution)/shard_map/convert_element_type | solution.py:39
  157.0 1.1 fusion.10
  158.1 1.0 copy.46
  (11 shorter events, 0.1 us)
Async XLA Ops:
  7.2 80.9 %all-gather.3.cloned.1.call-start = ((), (), s32[]{:S(2)}) async-start(), calls=%async_computation.2 | async-start | bytes 1179648 | tf_op jit(solution)/shard_map/all_gather | solution.py:42
  28.3 16.8 %copy-start.1 = (s32[1,16,8,4]{1,3,2,0:T(4,128)S(1)}, s32[1,16,8,4]{1,3,2,0:T(4,128)}, u32[]{:S(2)}) copy-start(s32[1,16,8,4]{1,3,2,0:T(4,128)} %param.9) | copy-start | bytes 6148
  45.0 112.0 %reduce-scatter.2.cloned.1.call-start = ((), (), s32[]{:S(2)}) async-start(), calls=%async_computation.1 | async-start | bytes 2621440 | tf_op jit(solution)/shard_map/reduce_scatter | solution.py:59
  111.6 9.0 %copy-start.2 = (bf16[1024,2048]{1,0:T(8,128)(2,1)S(1)}, bf16[1024,2048]{1,0:T(8,128)(2,1)}, u32[]{:S(2)}) copy-start(bf16[1024,2048]{1,0:T(8,128)(2,1)} %param.8) | copy-start | bytes 12582916
  118.6 2.0 %copy-start = (bf16[2048,1024]{1,0:T(8,128)(2,1)}, bf16[2048,1024]{1,0:T(8,128)(2,1)S(1)}, u32[]{:S(2)}) copy-start(bf16[2048,1024]{1,0:T(8,128)(2,1)S(1)} %fusion) | copy-start | bytes 12582916
Sparse Core Ops, SparseCore 0:
  45.1 42.9 all-gather.2
  126.5 30.2 reduce-scatter.1
where the time goes:
time: 167 us; the launch traced here: 166 us
  matrix products  52.6 us (31%)
  local copies, waits for them, and re-layouts  42.9 us (26%)
  blocking collectives  32.6 us (20%)
  between operations  14.1 us (8%)
  other arithmetic  13.7 us (8%)
  waiting for transfers between devices  9.98 us (6%)
    all_gather x1, blocking collectives, local(): lax.all_gather(chosen.astype(jnp.float32)[None].astype(jnp.bfloat16), 'wo...  32.6 us
    dot_general x1, matrix products, local(): jnp.einsum('abkr,akbc->arbc', rows_basis, partial_value, precision=HIGHES...  16.6 us
    dot_general x1, matrix products, local(): jnp.einsum('abkr,arbc->akbc', rows_basis, blended, precision=HIGHEST_PREC...  15.4 us
    convert_element_type x2, local copies, waits for them, and re-layouts, local(): (blended - decoded).reshape(local_rows, out_width).astype(jnp.bfloat16)  14 us
    all_gather x1, waiting for transfers between devices, local(): lax.all_gather(partial_value[None].astype(jnp.bfloat16), 'work', axis=0,...  9.95 us
    dot_general x1, matrix products, local(): jnp.einsum('rj,arbc->ajbc', transform, summed / workers, precision=HIGHES...  9.49 us
    add x1, local copies, waits for them, and re-layouts, local(): DECAY * momentum[0].astype(jnp.float32) + gradient[0].astype(jnp.float32)  9.29 us
    mul x1, local copies, waits for them, and re-layouts, local(): RATE * jnp.einsum('rj,arbc->ajbc', transform, summed / workers, precision...  9.28 us
  transfers between devices with their start and end apart: 2, of which 1 were waited for; matrix products, arithmetic and copies ran while one was open for 19% of the time, Pallas kernels for 0%

commit v1 on v0

v1 whole, which is shorter than its diff:
```python
import functools
import math

import jax
import jax.numpy as jnp
import ml_dtypes
import numpy as np
from jax import lax
from jax.experimental import pallas as pl
from jax.experimental.pallas import tpu as pltpu
from jax.sharding import PartitionSpec as P

TILE = 128
GROUP = 4
DECAY = 0.9
RATE = 8.0
BF16 = jnp.bfloat16
F32 = jnp.float32
MESH = pl.DeviceIdType.MESH


def cosine_basis():
    k = np.arange(TILE)[:, None].astype(np.float64)
    n = np.arange(TILE)[None, :].astype(np.float64)
    scale = np.where(k == 0, math.sqrt(1.0 / TILE), math.sqrt(2.0 / TILE))
    return scale * np.cos(math.pi * (2.0 * n + 1.0) * k / (2.0 * TILE))


def dot(a, b):
    return jnp.dot(a, b, preferred_element_type=F32)


def dot_nt(a, b):
    return lax.dot_general(a, b, (((1,), (1,)), ((), ())), preferred_element_type=F32)


def encode_kernel(nq, m_ref, g_ref, s_ref, basis_ref, basis_t_ref, out_ref, pv_ref, so_ref):
    step = pl.program_id(0)
    cols = m_ref.shape[2]
    ctiles = s_ref.shape[2]
    keep = s_ref.shape[3]
    per = keep * ctiles
    lane = lax.broadcasted_iota(jnp.int32, (ctiles, TILE), 1)

    @pl.when(step == 0)
    def _():
        so_ref[...] = jnp.zeros_like(so_ref)

    marks = []
    listed = so_ref[...]
    for i in range(GROUP):
        chosen = s_ref[0, i]
        for k in range(keep):
            wide = jnp.broadcast_to(chosen[:, k : k + 1], (ctiles, TILE))
            marks.append((wide == lane).astype(F32))
            listed = jnp.where(lane == (step * GROUP + i) * keep + k, wide.astype(F32), listed)
    so_ref[...] = listed
    onehot = jnp.concatenate(marks, axis=0).astype(BF16)
    rows = dot(onehot, basis_ref[...]).astype(BF16)
    rows_t = dot_nt(basis_t_ref[...], onehot).astype(BF16)

    row_id = lax.broadcasted_iota(jnp.int32, (per, cols), 0)
    col_id = lax.broadcasted_iota(jnp.int32, (per, cols), 1)
    own_tile = (row_id & (ctiles - 1)) == (col_id >> 7)
    kept = []
    for i in range(GROUP):
        at = slice(i * TILE, (i + 1) * TILE)
        blended = DECAY * m_ref[0, at].astype(F32) + g_ref[0, at].astype(F32)
        part = dot(rows[i * per : (i + 1) * per], blended.astype(BF16))
        kept.append(jnp.where(own_tile, part, 0.0).astype(BF16))
    kept = jnp.concatenate(kept, axis=0)

    fold_r = lax.broadcasted_iota(jnp.int32, (GROUP * keep, GROUP * per), 0)
    fold_c = lax.broadcasted_iota(jnp.int32, (GROUP * keep, GROUP * per), 1)
    fold = (fold_r == fold_c // ctiles).astype(F32).astype(BF16)
    compact = dot(fold, kept).astype(BF16)
    for c in range(ctiles):
        owner, q = c // nq, c % nq
        pv_ref[(owner // 2) * nq + q, owner % 2] = compact[:, c * TILE : (c + 1) * TILE]

    own_lane = lax.broadcasted_iota(jnp.int32, (TILE, GROUP * per), 1) // per
    for i in range(GROUP):
        at = slice(i * TILE, (i + 1) * TILE)
        blended = DECAY * m_ref[0, at].astype(F32) + g_ref[0, at].astype(F32)
        lhs = jnp.where(own_lane == i, rows_t, jnp.zeros_like(rows_t))
        out_ref[0, at] = (blended - dot(lhs, kept)).astype(BF16)


def mix_kernel(
    xs_n, ys_n, zs_n, nq, scale, feature_scale,
    pv_ref, so_ref, w_ref, t_ref, basis_t_ref,
    wout_ref, proj_ref,
    gat, selg, ohs, bsel, wv, tv, wo, own, cs, cr, xsend, xr,
    w_sem, t_sem, wo_sem, loc_sem, ag_send, ag_recv, c_send, c_recv, x_send, x_recv,
):
    feat, work = lax.axis_index("feat"), lax.axis_index("work")
    x, core = feat // 2, feat % 2
    z, y = work // ys_n, work % ys_n
    workers = ys_n * zs_n
    steps = xs_n * nq
    ak = gat.shape[3]
    groups = ak // 16
    span = workers * 16
    tokens = tv.shape[0]
    half = tokens // 2
    width = GROUP * TILE

    def zpeer(d):
        return lax.rem(z + d, zs_n) * ys_n + y

    def ypeer(d):
        return z * ys_n + lax.rem(y + d, ys_n)

    other_core = x * 2 + 1 - core

    def xpeer(d):
        return lax.rem(x + d, xs_n) * 2 + core

    def owner_x(s):
        return lax.rem(x + 1 + s // nq, xs_n)

    def tile_of(s, h):
        cc = core if h == 0 else 1 - core
        return (owner_x(s) * 2 + cc) * nq + s % nq

    loads = []
    for s in range(steps):
        for h in range(2):
            off = pl.multiple_of(tile_of(s, h) * TILE, TILE)
            loads.append(
                pltpu.make_async_copy(w_ref.at[:, pl.ds(off, TILE)], wv.at[s, h], w_sem.at[s, h])
            )
    load_t = pltpu.make_async_copy(t_ref, tv, t_sem.at[0])
    for s in range(steps + 1):
        src = so_ref if s == 0 else pv_ref.at[owner_x(s - 1) * nq + (s - 1) % nq]
        dst = selg.at[work] if s == 0 else gat.at[s - 1, work]
        pltpu.make_async_copy(src, dst, loc_sem.at[s]).start()

    barrier = pltpu.get_barrier_semaphore()
    count = 0
    for d in range(1, zs_n):
        pl.semaphore_signal(barrier, inc=1, device_id={"work": zpeer(d)}, device_id_type=MESH)
        count += 1
    for d in range(1, ys_n):
        pl.semaphore_signal(barrier, inc=1, device_id={"work": ypeer(d)}, device_id_type=MESH)
        count += 1
    pl.semaphore_signal(barrier, inc=1, device_id={"feat": other_core}, device_id_type=MESH)
    count += 1
    for d in range(1, xs_n):
        pl.semaphore_signal(barrier, inc=1, device_id={"feat": xpeer(d)}, device_id_type=MESH)
        count += 1
    pl.semaphore_wait(barrier, count)

    def source(r):
        return so_ref if r == 0 else pv_ref.at[owner_x(r - 1) * nq + (r - 1) % nq]

    def slot(r, w):
        return selg.at[w] if r == 0 else gat.at[r - 1, w]

    sent = []

    def push(r, src, w, to, which):
        copy = pltpu.make_async_remote_copy(
            src_ref=src, dst_ref=slot(r, w),
            send_sem=ag_send.at[r, which], recv_sem=ag_recv.at[r, w],
            device_id={"work": to}, device_id_type=MESH,
        )
        copy.start()
        sent.append(copy)

    def arrived(r, w):
        pltpu.make_async_remote_copy(
            src_ref=slot(r, w), dst_ref=slot(r, w),
            send_sem=ag_send.at[r, 0], recv_sem=ag_recv.at[r, w],
            device_id={"work": work}, device_id_type=MESH,
        ).wait_recv()

    def push_own(r):
        for d in range(1, zs_n):
            push(r, source(r), work, zpeer(d), d - 1)
        for e in range(1, ys_n):
            push(r, source(r), work, ypeer(e), zs_n - 1 + e - 1)

    def forward(r):
        base = zs_n - 1 + ys_n - 1
        for d in range(1, zs_n):
            w = zpeer(d)
            arrived(r, w)
            for e in range(1, ys_n):
                push(r, slot(r, w), w, ypeer(e), base + (d - 1) * (ys_n - 1) + e - 1)

    def rest(r):
        for e in range(1, ys_n):
            for d in range(zs_n):
                arrived(r, lax.rem(z + d, zs_n) * ys_n + lax.rem(y + e, ys_n))
        pltpu.make_async_copy(source(r), slot(r, work), loc_sem.at[r]).wait()

    for r in range(steps + 1):
        push_own(r)
    load_t.start()
    for copy in loads:
        copy.start()
    forward(0)
    forward(1)
    rest(0)

    ctiles = selg.shape[1]
    table = selg[...].reshape(workers * ctiles, TILE)
    fill = -table.shape[0] % TILE
    if fill:
        table = jnp.concatenate([table, jnp.zeros((fill, TILE), F32)], axis=0)
    table = table.T[:ak]
    lane = lax.broadcasted_iota(jnp.int32, (ak, TILE), 1).astype(F32)
    for w in range(workers):
        for c in range(ctiles):
            at = w * ctiles + c
            wide = jnp.broadcast_to(table[:, at : at + 1], (ak, TILE))
            hot = (wide == lane).astype(F32).astype(BF16)
            ohs[c, :, w * 16 : (w + 1) * 16, :] = hot.reshape(groups, 16, TILE)
    for c in range(ctiles):
        for g in range(groups):
            bsel[c, g] = dot_nt(basis_t_ref[...], ohs[c, g]).astype(BF16)

    part_of = (lax.broadcasted_iota(jnp.int32, (TILE, span), 1) >> 2) & (GROUP - 1)

    def decode(s):
        for h in range(2):
            cc = core if h == 0 else 1 - core
            c = tile_of(s, h)
            loads[s * 2 + h].wait()

            def body(g, carry):
                r16 = pl.multiple_of(g * 16, 16)
                rw = pl.multiple_of(g * width, width)
                values = gat[s, :, cc, pl.ds(r16, 16), :].reshape(span, TILE)
                vectors = bsel[c, g]
                lhs = jnp.concatenate(
                    [jnp.where(part_of == i, vectors, jnp.zeros_like(vectors)) for i in range(GROUP)],
                    axis=0,
                )
                update = dot(lhs, values)
                fresh = wv[s, h, pl.ds(rw, width), :].astype(F32) - scale * update
                wo[s, pl.ds(rw, width), h * TILE : (h + 1) * TILE] = fresh.astype(BF16)
                return carry

            lax.fori_loop(0, groups, body, 0)
            out_copy(s, h).start()

    def out_copy(s, h):
        off = pl.multiple_of(tile_of(s, h) * TILE, TILE)
        return pltpu.make_async_copy(
            wo.at[s, :, h * TILE : (h + 1) * TILE], wout_ref.at[:, pl.ds(off, TILE)], wo_sem.at[s, h]
        )

    def core_copy(s, p):
        at = slice(p * half, (p + 1) * half)
        return pltpu.make_async_remote_copy(
            src_ref=cs.at[s, at], dst_ref=cr.at[s, at],
            send_sem=c_send.at[s, p], recv_sem=c_recv.at[s, p],
            device_id={"feat": other_core}, device_id_type=MESH,
        )

    def x_copy(s, p):
        d = s // nq + 1
        at = slice(p * half, (p + 1) * half)
        return pltpu.make_async_remote_copy(
            src_ref=xsend.at[s, at], dst_ref=xr.at[s, at],
            send_sem=x_send.at[s, p], recv_sem=x_recv.at[s, p],
            device_id={"feat": xpeer(d)}, device_id_type=MESH,
        )

    block = min(256, half)

    def multiply(s, p):
        def body(t, carry):
            at = pl.ds(pl.multiple_of(p * half + t * block, block), block)
            both = dot(tv[at, :], wo[s])
            own[s, at, :] = both[:, :TILE]
            cs[s, at, :] = both[:, TILE:].astype(BF16)
            return carry

        lax.fori_loop(0, half // block, body, 0)
        core_copy(s, p).start()

    away = steps - nq

    def finish(s, p):
        at = slice(p * half, (p + 1) * half)
        core_copy(s, p).wait_recv()
        xsend[s, at] = (own[s, at] + cr[s, at].astype(F32)).astype(BF16)
        x_copy(s, p).start()

    for s in range(steps):
        rest(s + 1)
        decode(s)
        if s + 2 <= steps:
            forward(s + 2)
        if s == 0:
            load_t.wait()
        for p in range(2):
            multiply(s, p)
        if s < away:
            for p in range(2):
                finish(s, p)

    for q in range(nq):
        s = away + q
        for p in range(2):
            at = slice(p * half, (p + 1) * half)
            core_copy(s, p).wait_recv()
            total = own[s, at] + cr[s, at].astype(F32)
            for d in range(xs_n - 1):
                x_copy(d * nq + q, p).wait_recv()
                total = total + xr[d * nq + q, at].astype(F32)
            proj_ref[at, q * TILE : (q + 1) * TILE] = (total * feature_scale).astype(BF16)

    for copy in sent:
        copy.wait_send()
    for s in range(steps):
        for p in range(2):
            core_copy(s, p).wait_send()
            if s < away:
                x_copy(s, p).wait_send()
        for h in range(2):
            out_copy(s, h).wait()


def local(feats, momentum, gradient, weight, tokens, select):
    workers = lax.axis_size("work")
    rows, cols = weight.shape
    row_tiles, ctiles, keep = select.shape[1:]
    nq = ctiles // feats
    xs_n = feats // 2
    ys_n = xs_n if workers % xs_n == 0 else 1
    zs_n = workers // ys_n
    steps = xs_n * nq
    ak = row_tiles * keep
    count = tokens.shape[0]
    basis = cosine_basis()
    basis_c = jnp.asarray(basis.astype(ml_dtypes.bfloat16))
    basis_t = jnp.asarray(np.ascontiguousarray(basis.T).astype(ml_dtypes.bfloat16))
    height = GROUP * TILE

    moment_out, values, listed = pl.pallas_call(
        functools.partial(encode_kernel, nq),
        grid=(row_tiles // GROUP,),
        in_specs=[
            pl.BlockSpec((1, height, cols), lambda g: (0, g, 0)),
            pl.BlockSpec((1, height, cols), lambda g: (0, g, 0)),
            pl.BlockSpec((1, GROUP, ctiles, keep), lambda g: (0, g, 0, 0)),
            pl.BlockSpec((TILE, TILE), lambda g: (0, 0)),
            pl.BlockSpec((TILE, TILE), lambda g: (0, 0)),
        ],
        out_specs=[
            pl.BlockSpec((1, height, cols), lambda g: (0, g, 0)),
            pl.BlockSpec((steps, 2, 16, TILE), lambda g: (0, 0, g, 0)),
            pl.BlockSpec((ctiles, TILE), lambda g: (0, 0)),
        ],
        out_shape=[
            jax.ShapeDtypeStruct(momentum.shape, BF16),
            jax.ShapeDtypeStruct((steps, 2, ak, TILE), BF16),
            jax.ShapeDtypeStruct((ctiles, TILE), F32),
        ],
        compiler_params=pltpu.CompilerParams(vmem_limit_bytes=30 * 1024 * 1024),
        cost_estimate=pl.CostEstimate(flops=4 * rows * cols * 160, bytes_accessed=6 * rows * cols, transcendentals=0),
        name="encode",
    )(momentum, gradient, select, basis_c, basis_t)

    sends = (zs_n - 1) + zs_n * (ys_n - 1)
    away = steps - nq
    dma = pltpu.SemaphoreType.DMA
    anywhere = pl.BlockSpec(memory_space=pl.ANY)
    vmem = pl.BlockSpec(memory_space=pltpu.VMEM)
    weight_out, projected = pl.pallas_call(
        functools.partial(
            mix_kernel, xs_n, ys_n, zs_n, nq, RATE / workers, 1.0 / math.sqrt(rows * feats)
        ),
        in_specs=[anywhere, anywhere, anywhere, anywhere, vmem],
        out_specs=[anywhere, vmem],
        out_shape=[
            jax.ShapeDtypeStruct(weight.shape, BF16),
            jax.ShapeDtypeStruct((count, cols // feats), BF16),
        ],
        scratch_shapes=[
            pltpu.VMEM((steps, workers, 2, ak, TILE), BF16),
            pltpu.VMEM((workers, ctiles, TILE), F32),
            pltpu.VMEM((ctiles, ak // 16, workers * 16, TILE), BF16),
            pltpu.VMEM((ctiles, ak // 16, TILE, workers * 16), BF16),
            pltpu.VMEM((steps, 2, rows, TILE), BF16),
            pltpu.VMEM((count, rows), BF16),
            pltpu.VMEM((steps, rows, 2 * TILE), BF16),
            pltpu.VMEM((steps, count, TILE), F32),
            pltpu.VMEM((steps, count, TILE), BF16),
            pltpu.VMEM((steps, count, TILE), BF16),
            pltpu.VMEM((away, count, TILE), BF16),
            pltpu.VMEM((away, count, TILE), BF16),
            dma((steps, 2)),
            dma((1,)),
            dma((steps, 2)),
            dma((steps + 1,)),
            dma((steps + 1, sends)),
            dma((steps + 1, workers)),
            dma((steps, 2)),
            dma((steps, 2)),
            dma((away, 2)),
            dma((away, 2)),
        ],
        compiler_params=pltpu.CompilerParams(
            collective_id=0, has_side_effects=True, vmem_limit_bytes=40 * 1024 * 1024
        ),
        cost_estimate=pl.CostEstimate(
            flops=2 * count * rows * cols, bytes_accessed=20 * 1024 * 1024, transcendentals=0
        ),
        name="mix",
    )(values, listed, weight, tokens, basis_t)
    return (moment_out, weight_out, projected)


def solution(mesh):
    in_specs = (
        P("work", "feat", None),
        P("work", "feat", None),
        P("feat", None),
        P("work", "feat"),
        P("work", "feat", None, None),
    )
    out_specs = (P("work", "feat", None), P("feat", None), P("work", "feat"))
    return jax.shard_map(
        functools.partial(local, mesh.shape["feat"]),
        mesh=mesh, in_specs=in_specs, out_specs=out_specs, check_vma=False,
    )
```

time: 167 us -> 52.6 us (0.31)
  the two profiles are of different devices: /device:TPU:0 before, /device:TPU:9 now
where the time goes in v1:
time: 52.6 us; the launch traced here: 52.2 us
  Pallas kernels  42 us (80%)
  local copies, waits for them, and re-layouts  9.55 us (18%)
  between operations  0.65 us (1%)
    pallas_call x1, Pallas kernels, local(): pl.pallas_call(functools.partial(mix_kernel, xs_n, ys_n, zs_n, nq, RATE /...  36.9 us
    unnamed x17, local copies, waits for them, and re-layouts  9.55 us
    pallas_call x1, Pallas kernels, local(): pl.pallas_call(functools.partial(encode_kernel, nq), grid=(row_tiles // G...  5.09 us

profile of v1, /device:TPU:9, one launch (start us, length us, event | category | flops | bytes accessed | tf_op | source)
XLA Modules:
  0.0 52.2 jit_solution(11319802757808691426)
XLA Ops:
  0.6 0.8 %copy.10.s_ref = s32[1,16,8,4]{3,2,1,0:T(8,128)S(1)} copy(s32[1,16,8,4]{1,3,2,0:T(4,128)} %param.11) | data formatting | bytes 4096 | tf_op args[4]
  1.5 0.0 copy-start
  1.5 2.2 %copy-done = bf16[1,2048,1024]{2,1,0:T(8,128)(2,1)S(1)} copy-done((bf16[1,2048,1024]{2,1,0:T(8,128)(2,1)S(1)}, bf16[1,2048,1024]{2,1,0:T(8,128)(2,1)}, u32[]{:S(2)}) %copy-start) | copy-done | bytes 4194328
  3.7 0.0 copy-start.1
  3.7 2.2 %copy-done.1 = bf16[1,2048,1024]{2,1,0:T(8,128)(2,1)S(1)} copy-done((bf16[1,2048,1024]{2,1,0:T(8,128)(2,1)S(1)}, bf16[1,2048,1024]{2,1,0:T(8,128)(2,1)}, u32[]{:S(2)}) %copy-start.1) | copy-done | bytes 4194328
  5.8 0.0 copy-start.2
  5.9 0.8 %copy-done.2 = bf16[128,128]{1,0:T(8,128)(2,1)S(1)} copy-done((bf16[128,128]{1,0:T(8,128)(2,1)S(1)}, bf16[128,128]{1,0:T(8,128)(2,1)}, u32[]{:S(2)}) %copy-start.2) | copy-done | bytes 32792
  6.6 0.0 copy-start.4
  6.6 0.8 %copy-done.4 = bf16[128,128]{1,0:T(8,128)(2,1)S(1)} copy-done((bf16[128,128]{1,0:T(8,128)(2,1)S(1)}, bf16[128,128]{1,0:T(8,128)(2,1)}, u32[]{:S(2)}) %copy-start.4) | copy-done | bytes 32792
  7.4 0.0 copy-start.3
  7.4 0.0 copy-start.5
  7.4 0.0 copy-start.6
  7.4 5.1 %encode.1 = (bf16[1,2048,1024]{2,1,0:T(8,128)(2,1)}, bf16[4,2,64,128]{3,2,1,0:T(8,128)(2,1)S(1)}, f32[8,128]{1,0:T(8,128)S(1)}) custom-call(bf16[1,2048,1024]{2,1,0:T(8,128)(2,1)S(1)} %copy-done, bf16[1,2048,1024]{2,1,0:T(8,128)(2,1)S(1)} %copy-done.1, s32[1,16,8,4]{3,2,1,0:T(8,128)S(1)} %copy.10.s_ref, bf16[128,128]{1,0:T(8,128)(2,1)S(1)} %copy-done.4, ...), custom_call_target="tpu_custom_call" | custom-call | flops 1342177280 | bytes 12582912 | tf_op jit(solution)/shard_map/encode/pallas_call | solution.py:344
  12.5 0.0 copy-done.3
  12.5 0.0 copy-done.5
  12.5 0.0 copy-done.6
  12.5 36.9 %mix.1 = (bf16[2048,1024]{1,0:T(8,128)(2,1)S(1)}, bf16[1024,256]{1,0:T(8,128)(2,1)S(1)}) custom-call(bf16[4,2,64,128]{3,2,1,0:T(8,128)(2,1)S(1)} %get-tuple-element.9.pv_ref, f32[8,128]{1,0:T(8,128)S(1)} %get-tuple-element.10.so_ref, bf16[2048,1024]{1,0:T(8,128)(2,1)S(1)} %copy-done.5, bf16[1024,2048]{1,0:T(8,128)(2,1)S(1)} %copy-done.6, ...), custom_call_target="tpu_custom_call" | custom-call | flops 4294967296 | bytes 20971520 | tf_op jit(solution)/shard_map/mix/pallas_call | solution.py:374
  49.4 2.0 %copy.13 = bf16[2048,1024]{1,0:T(8,128)(2,1)} copy(bf16[2048,1024]{1,0:T(8,128)(2,1)S(1)} %get-tuple-element.17) | data formatting | bytes 8388608
  51.4 0.8 %copy.14 = bf16[1024,256]{1,0:T(8,128)(2,1)} copy(bf16[1024,256]{1,0:T(8,128)(2,1)S(1)} %get-tuple-element.18) | data formatting | bytes 1048576
Async XLA Ops:
  1.5 2.2 %copy-start = (bf16[1,2048,1024]{2,1,0:T(8,128)(2,1)S(1)}, bf16[1,2048,1024]{2,1,0:T(8,128)(2,1)}, u32[]{:S(2)}) copy-start(bf16[1,2048,1024]{2,1,0:T(8,128)(2,1)} %m_ref.1) | copy-start | bytes 12582916
  3.7 2.2 %copy-start.1 = (bf16[1,2048,1024]{2,1,0:T(8,128)(2,1)S(1)}, bf16[1,2048,1024]{2,1,0:T(8,128)(2,1)}, u32[]{:S(2)}) copy-start(bf16[1,2048,1024]{2,1,0:T(8,128)(2,1)} %g_ref.1) | copy-start | bytes 12582916
  5.8 0.8 %copy-start.2 = (bf16[128,128]{1,0:T(8,128)(2,1)S(1)}, bf16[128,128]{1,0:T(8,128)(2,1)}, u32[]{:S(2)}) copy-start(bf16[128,128]{1,0:T(8,128)(2,1)} %constant.5.clone.basis_t_ref) | copy-start | bytes 98308
  6.6 0.8 %copy-start.4 = (bf16[128,128]{1,0:T(8,128)(2,1)S(1)}, bf16[128,128]{1,0:T(8,128)(2,1)}, u32[]{:S(2)}) copy-start(bf16[128,128]{1,0:T(8,128)(2,1)} %constant.4.clone.basis_ref) | copy-start | bytes 98308
  7.4 5.1 %copy-start.3 = (bf16[128,128]{1,0:T(8,128)(2,1)S(1)}, bf16[128,128]{1,0:T(8,128)(2,1)}, u32[]{:S(2)}) copy-start(bf16[128,128]{1,0:T(8,128)(2,1)} %constant.5.clone.basis_t_ref) | copy-start | bytes 98308
  7.4 5.1 %copy-start.5 = (bf16[2048,1024]{1,0:T(8,128)(2,1)S(1)}, bf16[2048,1024]{1,0:T(8,128)(2,1)}, u32[]{:S(2)}) copy-start(bf16[2048,1024]{1,0:T(8,128)(2,1)} %w_ref.1) | copy-start | bytes 12582916
  7.4 5.1 %copy-start.6 = (bf16[1024,2048]{1,0:T(8,128)(2,1)S(1)}, bf16[1024,2048]{1,0:T(8,128)(2,1)}, u32[]{:S(2)}) copy-start(bf16[1024,2048]{1,0:T(8,128)(2,1)} %t_ref.1) | copy-start | bytes 12582916

commit v2 on v1

--- a/solution.py
+++ b/solution.py
@@ -65,8 +65,8 @@
     kept = []
     for i in range(GROUP):
         at = slice(i * TILE, (i + 1) * TILE)
-        blended = DECAY * m_ref[0, at].astype(F32) + g_ref[0, at].astype(F32)
-        part = dot(rows[i * per : (i + 1) * per], blended.astype(BF16))
+        chosen_rows = rows[i * per : (i + 1) * per]
+        part = DECAY * dot(chosen_rows, m_ref[0, at]) + dot(chosen_rows, g_ref[0, at])
         kept.append(jnp.where(own_tile, part, 0.0).astype(BF16))
     kept = jnp.concatenate(kept, axis=0)
 
@@ -188,6 +188,8 @@
             arrived(r, w)
             for e in range(1, ys_n):
                 push(r, slot(r, w), w, ypeer(e), base + (d - 1) * (ys_n - 1) + e - 1)
+        if r + 2 <= steps:
+            push_own(r + 2)
 
     def rest(r):
         for e in range(1, ys_n):
@@ -195,13 +197,12 @@
                 arrived(r, lax.rem(z + d, zs_n) * ys_n + lax.rem(y + e, ys_n))
         pltpu.make_async_copy(source(r), slot(r, work), loc_sem.at[r]).wait()
 
-    for r in range(steps + 1):
-        push_own(r)
-    load_t.start()
+    push_own(0)
+    push_own(1)
     for copy in loads:
         copy.start()
+    load_t.start()
     forward(0)
-    forward(1)
     rest(0)
 
     ctiles = selg.shape[1]
@@ -217,6 +218,7 @@
             wide = jnp.broadcast_to(table[:, at : at + 1], (ak, TILE))
             hot = (wide == lane).astype(F32).astype(BF16)
             ohs[c, :, w * 16 : (w + 1) * 16, :] = hot.reshape(groups, 16, TILE)
+    forward(1)
     for c in range(ctiles):
         for g in range(groups):
             bsel[c, g] = dot_nt(basis_t_ref[...], ohs[c, g]).astype(BF16)
@@ -243,7 +245,7 @@
                 wo[s, pl.ds(rw, width), h * TILE : (h + 1) * TILE] = fresh.astype(BF16)
                 return carry
 
-            lax.fori_loop(0, groups, body, 0)
+            lax.fori_loop(0, groups, body, 0, unroll=True)
             out_copy(s, h).start()
 
     def out_copy(s, h):
@@ -269,7 +271,7 @@
             device_id={"feat": xpeer(d)}, device_id_type=MESH,
         )
 
-    block = min(256, half)
+    block = half
 
     def multiply(s, p):
         def body(t, carry):
@@ -292,13 +294,15 @@
 
     for s in range(steps):
         rest(s + 1)
+        if s == 0:
+            forward(2)
         decode(s)
-        if s + 2 <= steps:
-            forward(s + 2)
         if s == 0:
             load_t.wait()
-        for p in range(2):
-            multiply(s, p)
+        multiply(s, 0)
+        if s + 3 <= steps:
+            forward(s + 3)
+        multiply(s, 1)
         if s < away:
             for p in range(2):
                 finish(s, p)
@@ -361,7 +365,7 @@
             jax.ShapeDtypeStruct((steps, 2, ak, TILE), BF16),
             jax.ShapeDtypeStruct((ctiles, TILE), F32),
         ],
-        compiler_params=pltpu.CompilerParams(vmem_limit_bytes=30 * 1024 * 1024),
+        compiler_params=pltpu.CompilerParams(vmem_limit_bytes=58 * 1024 * 1024),
         cost_estimate=pl.CostEstimate(flops=4 * rows * cols * 160, bytes_accessed=6 * rows * cols, transcendentals=0),
         name="encode",
     )(momentum, gradient, select, basis_c, basis_t)
@@ -371,14 +375,15 @@
     dma = pltpu.SemaphoreType.DMA
     anywhere = pl.BlockSpec(memory_space=pl.ANY)
     vmem = pl.BlockSpec(memory_space=pltpu.VMEM)
+    hbm = pl.BlockSpec(memory_space=pltpu.HBM)
     weight_out, projected = pl.pallas_call(
         functools.partial(
             mix_kernel, xs_n, ys_n, zs_n, nq, RATE / workers, 1.0 / math.sqrt(rows * feats)
         ),
-        in_specs=[anywhere, anywhere, anywhere, anywhere, vmem],
+        in_specs=[anywhere, anywhere, hbm, hbm, vmem],
         out_specs=[anywhere, vmem],
         out_shape=[
-            jax.ShapeDtypeStruct(weight.shape, BF16),
+            pltpu.VMEM(weight.shape, BF16),
             jax.ShapeDtypeStruct((count, cols // feats), BF16),
         ],
         scratch_shapes=[
@@ -406,7 +411,7 @@
             dma((away, 2)),
         ],
         compiler_params=pltpu.CompilerParams(
-            collective_id=0, has_side_effects=True, vmem_limit_bytes=40 * 1024 * 1024
+            collective_id=0, has_side_effects=True, vmem_limit_bytes=58 * 1024 * 1024
         ),
         cost_estimate=pl.CostEstimate(
             flops=2 * count * rows * cols, bytes_accessed=20 * 1024 * 1024, transcendentals=0

time: 52.6 us -> 48.9 us (0.930)
  the two profiles are of different devices: /device:TPU:9 before, /device:TPU:0 now
where the time goes in v2:
time: 48.9 us; the launch traced here: 48.6 us
  Pallas kernels  43.7 us (89%)
  local copies, waits for them, and re-layouts  4.28 us (9%)
  between operations  0.65 us (1%)
    pallas_call x1, Pallas kernels, local(): pl.pallas_call(functools.partial(mix_kernel, xs_n, ys_n, zs_n, nq, RATE /...  35.7 us
    pallas_call x1, Pallas kernels, local(): pl.pallas_call(functools.partial(encode_kernel, nq), grid=(row_tiles // G...  7.98 us
    unnamed x5, local copies, waits for them, and re-layouts  4.28 us

profile of v2, /device:TPU:0, one launch (start us, length us, event | category | flops | bytes accessed | tf_op | source)
XLA Modules:
  0.0 48.6 jit_solution(2129914147239433527)
XLA Ops:
  0.6 1.5 %copy.10.s_ref = s32[1,16,8,4]{3,2,1,0:T(8,128)} copy(s32[1,16,8,4]{1,3,2,0:T(4,128)} %param.11) | data formatting | bytes 4096 | tf_op args[4]
  2.1 8.0 %encode.1 = (bf16[1,2048,1024]{2,1,0:T(8,128)(2,1)}, bf16[4,2,64,128]{3,2,1,0:T(8,128)(2,1)}, f32[8,128]{1,0:T(8,128)}) custom-call(bf16[1,2048,1024]{2,1,0:T(8,128)(2,1)} %m_ref.1, bf16[1,2048,1024]{2,1,0:T(8,128)(2,1)} %g_ref.1, s32[1,16,8,4]{3,2,1,0:T(8,128)} %copy.10.s_ref, bf16[128,128]{1,0:T(8,128)(2,1)} %constant.4.clone.basis_ref, ...), custom_call_target="tpu_custom_call" | custom-call | flops 1342177280 | bytes 12582912 | tf_op jit(solution)/shard_map/encode/pallas_call | solution.py:348
  10.1 35.7 %mix.1 = (bf16[2048,1024]{1,0:T(8,128)(2,1)S(1)}, bf16[1024,256]{1,0:T(8,128)(2,1)}) custom-call(bf16[4,2,64,128]{3,2,1,0:T(8,128)(2,1)} %get-tuple-element.9.pv_ref, f32[8,128]{1,0:T(8,128)} %get-tuple-element.10.so_ref, bf16[2048,1024]{1,0:T(8,128)(2,1)} %w_ref.1, bf16[1024,2048]{1,0:T(8,128)(2,1)} %t_ref.1, bf16[128,128]{1,0:T(8,128)(2,1)} %constant.5.clone.basis_t_ref), custom_call_target="tpu_custom_call" | custom-call | flops 4294967296 | bytes 20971520 | tf_op jit(solution)/shard_map/mix/pallas_call | solution.py:379
  45.8 0.0 copy-start
  45.8 2.0 %copy.13 = bf16[2048,1024]{1,0:T(8,128)(2,1)} copy(bf16[2048,1024]{1,0:T(8,128)(2,1)S(1)} %get-tuple-element.14) | data formatting | bytes 8388608
  47.8 0.0 copy-done
  47.9 0.8 %copy.14 = bf16[1024,256]{1,0:T(8,128)(2,1)} copy(bf16[1024,256]{1,0:T(8,128)(2,1)S(1)} %copy-done) | data formatting | bytes 1048576
Async XLA Ops:
  45.8 2.0 %copy-start = (bf16[1024,256]{1,0:T(8,128)(2,1)S(1)}, bf16[1024,256]{1,0:T(8,128)(2,1)}, u32[]{:S(2)}) copy-start(bf16[1024,256]{1,0:T(8,128)(2,1)} %get-tuple-element.21) | copy-start | bytes 1572868
